TPU v7x, 512 devices: a whole 4x8x8 slice. The times are simulated.
512 devices in a mesh: img: 32 (over y, z_lo, core), rows: 16 (over z_hi, x).
Axes of the slice: x: 4, y: 8, z: 8 (z_hi: 4, z_lo: 2; z = z_hi * 2 + z_lo), core: 2. Of those that a mesh axis runs over, the one named last changes fastest.
Arguments:
- center_mid: bfloat16 [32, 64, 32, 512], P('img', 'rows'), may hold values from -6 to 6
- radius_mid: bfloat16 [32, 64, 32, 512], P('img', 'rows'), may hold values from 0.049804688 to 1.5
- conv_weight: bfloat16 [512, 3, 3, 512], P('img'), may hold values from -0.09375 to 0.09375
- center_upstream: bfloat16 [32, 64, 32, 512], P('img', 'rows'), may hold values from -6 to 6
- radius_upstream: bfloat16 [32, 64, 32, 512], P('img', 'rows'), may hold values from -6 to 6
Outputs:
- center_mid_grad: bfloat16 [32, 64, 32, 512], P('img', 'rows')
- radius_mid_grad: bfloat16 [32, 64, 32, 512], P('img', 'rows')
- weight_grad: float32 [512, 3, 3, 512], P('img', None, None, 'rows')
All inputs are finite; a program needn't handle non-finite values.
Results may differ from a plain program's by a relative error of at most 0.0055.
Values may be sent and summed in bfloat16 or wider, within the bound.
A program may use at most 64 MiB of HBM per device.

v0:
```python
import jax
import jax.numpy as jnp
from jax import lax
from jax.sharding import PartitionSpec as P


def with_halo(cells, sides, width):
    for axis, dim in sides:
        count = lax.axis_size(axis)
        ends = count - 1
        head = lax.slice_in_dim(cells, 0, width, axis=dim)
        tail = lax.slice_in_dim(cells, cells.shape[dim] - width, cells.shape[dim], axis=dim)
        cells = jnp.concatenate(
            [
                lax.ppermute(tail, axis, [(i, (i + 1) % count) for i in range(ends)]),
                cells,
                lax.ppermute(head, axis, [((i + 1) % count, i) for i in range(ends)]),
            ],
            axis=dim,
        )
    return cells


def pad_columns(block):
    widths = [(0, 0)] * (block.ndim - 2) + [(1, 1), (0, 0)]
    return jnp.pad(block, widths)


def tap_product(left, kernel_tap):
    return lax.dot_general(
        left, kernel_tap, (((left.ndim - 1,), (1,)), ((), ())), preferred_element_type=jnp.float32
    )


def weight_terms(inputs_pad, piece, row_count, col_count):
    terms = []
    for tap_row in range(3):
        for tap_col in range(3):
            window = inputs_pad[
                :, :, tap_row : tap_row + row_count, tap_col : tap_col + col_count, :
            ]
            terms.append(
                lax.dot_general(
                    window,
                    piece,
                    (((1, 2, 3), (1, 2, 3)), ((0,), (0,))),
                    preferred_element_type=jnp.float32,
                )
            )
    stacked = jnp.stack(terms, axis=2)
    return stacked.reshape(stacked.shape[0], stacked.shape[1], 3, 3, stacked.shape[3])


def data_padded(padded, kernel, row_count, col_count):
    total = None
    for tap_row in range(3):
        for tap_col in range(3):
            window = padded[
                :, 2 - tap_row : 2 - tap_row + row_count, 2 - tap_col : 2 - tap_col + col_count, :
            ]
            term = tap_product(window, kernel[:, tap_row, tap_col, :])
            total = term if total is None else total + term
    return total


def layer_back(upstream, weight, inputs_pad):
    row_count = upstream.shape[2]
    col_count = upstream.shape[3]
    batch = inputs_pad.shape[1]
    kernels = (weight, jnp.abs(weight))
    operand = with_halo(upstream, (("rows", 2),), 1)
    padded = pad_columns(lax.all_gather(operand, "img", axis=1, tiled=True))
    inner = padded[:, :, 1 : row_count + 1, 1 : col_count + 1, :]
    running = weight_terms(inputs_pad, inner, row_count, col_count)
    fresh = jnp.stack(
        [data_padded(padded[which], kernels[which], row_count, col_count) for which in range(2)]
    )
    grads = fresh.astype(jnp.bfloat16)
    running, grads = (running, grads)
    image_cot = lax.all_to_all(grads, "img", split_axis=1, concat_axis=4, tiled=True)
    partial_value = (running[0] + jnp.sign(weight.astype(jnp.float32)) * running[1]) / batch
    summed = lax.psum_scatter(partial_value, "rows", scatter_dimension=3, tiled=True)
    return (image_cot, summed)


def on_device(center_mid, radius_mid, conv_weight, center_upstream, radius_upstream):
    stored = jnp.stack([center_mid, radius_mid])
    channel = lax.all_to_all(stored, "img", split_axis=4, concat_axis=1, tiled=True)
    rimmed = with_halo(channel, (("rows", 2),), 1)
    rimmed = pad_columns(rimmed)
    middle = rimmed[0].astype(jnp.float32)
    spread = rimmed[1].astype(jnp.float32)
    act_upper = jnp.maximum(middle + spread, 0.0)
    act_lower = jnp.maximum(middle - spread, 0.0)
    hidden_pad = jnp.stack([(act_upper + act_lower) * 0.5, (act_upper - act_lower) * 0.5]).astype(
        jnp.bfloat16
    )
    upstream = jnp.stack([center_upstream, radius_upstream])
    hidden_cot, weight_grad = layer_back(upstream, conv_weight, hidden_pad)
    upper_on = (center_mid > -radius_mid).astype(jnp.float32)
    lower_on = (center_mid > radius_mid).astype(jnp.float32)
    center_part = hidden_cot[0].astype(jnp.float32)
    radius_part = hidden_cot[1].astype(jnp.float32)
    upper_cot = 0.5 * (center_part + radius_part) * upper_on
    lower_cot = 0.5 * (center_part - radius_part) * lower_on
    center_mid_grad = (upper_cot + lower_cot).astype(jnp.bfloat16)
    radius_mid_grad = (upper_cot - lower_cot).astype(jnp.bfloat16)
    return (center_mid_grad, radius_mid_grad, weight_grad)


def solution(mesh):
    placed = (
        P("img", "rows", None, None),
        P("img", "rows", None, None),
        P("img", None, None, None),
        P("img", "rows", None, None),
        P("img", "rows", None, None),
    )
    return jax.shard_map(
        on_device,
        mesh=mesh,
        in_specs=placed,
        out_specs=(
            P("img", "rows", None, None),
            P("img", "rows", None, None),
            P("img", None, None, "rows"),
        ),
        check_vma=False,
    )
```

profile of v0, /device:TPU:8, one launch (start us, length us, event | category | flops | bytes accessed | tf_op | source)
XLA Modules:
  0.0 319.0 jit_solution(3447518856735842004)
XLA Ops:
  7.2 0.9 pad_maximum_fusion.6
  8.2 3.4 %collective-permute-start = (bf16[2,1,1,32,512]{4,3,2,1,0:T(8,128)(2,1)S(1)}, bf16[2,1,1,32,512]{4,3,2,1,0:T(8,128)(2,1)S(1)}, u32[]{:S(2)}, u32[]{:S(2)}) collective-permute-start(bf16[2,1,1,32,512]{4,3,2,1,0:T(8,128)(2,1)S(1)} %get-tuple-element.21), channel_id=1, source_target_pairs={{0,1},{1,2},{2,3},{3,4},{4,5},{5,6},{6,7},{7,8},{8,9},{9,10},{10,1... | collective-permute-start | bytes 196616 | tf_op jit(solution)/shard_map/ppermute | solution.py:15
  11.6 1.3 collective-permute-start.1
  12.9 0.6 collective-permute-done
  13.5 4.3 %collective-permute-done.1 = bf16[2,1,1,32,512]{4,3,2,1,0:T(8,128)(2,1)S(1)} collective-permute-done((bf16[2,1,1,32,512]{4,3,2,1,0:T(8,128)(2,1)S(1)}, bf16[2,1,1,32,512]{4,3,2,1,0:T(8,128)(2,1)S(1)}, u32[]{:S(2)}, u32[]{:S(2)}) %collective-permute-start.1) | collective-permute-done | bytes 65568 | tf_op jit(solution)/shard_map/ppermute | solution.py:17
  17.7 1.8 pad_maximum_fusion.3
  19.5 1.0 pad_maximum_fusion.4
  20.5 0.7 copy.26
  21.2 1.0 reshape.102
  22.3 20.8 %all_to_all.33 = bf16[32,2,2048]{2,1,0:T(2,128)(2,1)S(1)} all-to-all(bf16[32,2,2048]{2,1,0:T(2,128)(2,1)S(1)} %reshape.102), channel_id=1, replica_groups=mesh['img'=32,'rows'=16] {'img'}, dimensions={0} | all-to-all | bytes 524288 | tf_op jit(solution)/shard_map/all_to_all | solution.py:88
  43.1 0.5 reshape.103
  43.6 0.3 copy.91
  43.9 3.4 %collective-permute-start.2 = (bf16[2,32,1,32,16]{3,4,2,0,1:T(8,128)(2,1)S(1)}, bf16[2,32,1,32,16]{3,4,2,0,1:T(8,128)(2,1)S(1)}, u32[]{:S(2)}, u32[]{:S(2)}) collective-permute-start(bf16[2,32,1,32,16]{3,4,2,0,1:T(8,128)(2,1)S(1)} %get-tuple-element.15), channel_id=1, source_target_pairs={{0,1},{1,2},{2,3},{3,4},{4,5},{5,6},{6,7},{7,8},{8,9},{9,10},{10,1... | collective-permute-start | bytes 196616 | tf_op jit(solution)/shard_map/ppermute | solution.py:15
  47.3 1.3 collective-permute-start.3
  48.7 1.0 copy.19
  49.7 1.1 copy.20
  50.8 1.8 collective-permute-done.2
  52.6 5.7 %collective-permute-done.3 = bf16[2,32,1,32,16]{3,4,2,0,1:T(8,128)(2,1)S(1)} collective-permute-done((bf16[2,32,1,32,16]{3,4,2,0,1:T(8,128)(2,1)S(1)}, bf16[2,32,1,32,16]{3,4,2,0,1:T(8,128)(2,1)S(1)}, u32[]{:S(2)}, u32[]{:S(2)}) %collective-permute-start.3) | collective-permute-done | bytes 65568 | tf_op jit(solution)/shard_map/ppermute | solution.py:17
  58.2 0.8 fusion.43
  59.1 0.6 multiply_convert_fusion
  59.7 55.6 %all-gather.2.cloned.1.call-done = bf16[2,32,6,32,512]{4,3,2,1,0:T(8,128)(2,1)} async-done(((bf16[2,1,6,32,512]{4,3,2,1,0:T(8,128)(2,1)}), bf16[2,32,6,32,512]{4,3,2,1,0:T(8,128)(2,1)}) %all-gather.2.cloned.1.call-update) | async-done | bytes 12582928 | tf_op jit(solution)/shard_map/all_gather | solution.py:72
  115.3 10.8 %fusion = (bf16[32,6,34,512]{3,2,1,0:T(8,128)(2,1)S(1)}, bf16[32,6,34,512]{3,2,1,0:T(8,128)(2,1)S(1)}) fusion(bf16[2,32,6,32,512]{4,3,2,1,0:T(8,128)(2,1)} %all-gather.2.cloned.1.call-done), kind=kLoop, calls=%fused_computation.2 | loop fusion | bytes 25952256 | tf_op jit(solution)/shard_map/squeeze | solution.py:76
  126.1 2.8 fusion.34
  128.9 2.8 fusion.28
  131.8 2.8 fusion.30
  134.6 2.8 fusion.22
  137.5 2.8 fusion.24
  140.3 3.1 fusion.16
  143.4 2.8 fusion.10
  146.2 2.8 fusion.12
  149.1 2.8 fusion.4
  151.9 2.8 fusion.6
  154.7 2.9 fusion.88
  157.6 3.3 %fusion.85 = f32[32,4,32,16]{2,3,1,0:T(8,128)S(1)} fusion(f32[32,4,32,16]{2,3,1,0:T(8,128)S(1)} %fusion.28, f32[32,4,32,16]{2,3,1,0:T(8,128)S(1)} %fusion.30, f32[32,4,32,16]{2,3,1,0:T(8,128)S(1)} %fusion.88, bf16[32,6,34,512]{3,2,1,0:T(8,128)(2,1)S(1)} %get-tuple-element.9, bf16[16,3,3,512]{3,0,2,1:T(8,128)(2,1)S(1)} %copy-done.2), kind=kOutput, calls=%fused_computation.83 | convolution fusion | flops 67305472 | bytes 7618560 | tf_op jit(solution)/shard_map/dot_general | solution.py:30
  160.9 2.9 fusion.79
  163.8 2.8 fusion.100
  166.6 2.8 fusion.91
  169.5 2.9 fusion.73
  172.4 2.9 fusion.67
  175.3 2.9 fusion.103
  178.1 0.3 copy_bitcast_fusion.1
  178.4 1.7 reshape.100
  180.2 5.5 %all-to-all-start = ((bf16[32,2,2048]{2,1,0:T(2,128)(2,1)}), bf16[32,2,2048]{2,1,0:T(2,128)(2,1)}, u32[]{:S(2)}, u32[]{:S(2)}) async-start(bf16[32,2,2048]{2,1,0:T(2,128)(2,1)} %reshape.100), calls=%async_computation | async-start | bytes 524288 | tf_op jit(solution)/shard_map/all_to_all | solution.py:80
  185.7 4.6 %fusion.114 = f32[2,16,9,512]{3,1,0,2:T(8,128)S(1)} fusion(bf16[1,32,6,34,16]{3,4,2,0,1:T(8,128)(2,1)S(1)} %get-tuple-element.14, bf16[1,32,6,34,16]{3,4,2,0,1:T(8,128)(2,1)S(1)} %get-tuple-element.13, bf16[2,32,6,32,512]{4,3,2,1,0:T(8,128)(2,1)} %all-gather.2.cloned.1.call-done), kind=kOutput, calls=%fused_computation.109 | convolution fusion | flops 134348800 | bytes 8871936 | tf_op jit(solution)/shard_map/dot_general | solution.py:43
  190.3 4.9 %fusion.113 = f32[2,16,9,512]{3,1,0,2:T(8,128)S(1)} fusion(f32[2,16,9,512]{3,1,0,2:T(8,128)S(1)} %fusion.114, bf16[1,32,6,34,16]{3,4,2,0,1:T(8,128)(2,1)S(1)} %get-tuple-element.14, bf16[1,32,6,34,16]{3,4,2,0,1:T(8,128)(2,1)S(1)} %get-tuple-element.13, bf16[2,32,6,32,512]{4,3,2,1,0:T(8,128)(2,1)} %all-gather.2.cloned.1.call-done), kind=kOutput, calls=%fused_computation.107 | convolution fusion | flops 134348800 | bytes 10027008 | tf_op jit(solution)/shard_map/dot_general | solution.py:43
  195.2 0.3 slice-done.2
  195.5 1.9 fusion.112
  197.4 1.4 fusion.111
  198.8 1.9 fusion.110
  200.7 1.9 fusion.109
  202.6 1.5 fusion.108
  204.1 1.9 fusion.107
  206.0 1.9 fusion.106
  208.0 1.5 copy.69
  209.5 2.1 reshape.98
  211.7 2.0 reshape.101
  213.7 0.3 bitcast_bitcast_fusion
  214.0 0.3 fusion.115
  214.5 0.4 subtract_convert_fusion
  214.9 0.8 copy.38
  215.8 0.8 copy.39
  216.6 93.7 %reduce-scatter.4.cloned.1.call-done = f32[32,144]{1,0:T(8,128)} async-done(((f32[512,144]{1,0:T(8,128)}), f32[32,144]{1,0:T(8,128)}) %reduce-scatter.4.cloned.1.call-update) | async-done | bytes 18448
  310.4 0.9 reshape.99
  311.3 0.8 copy.70
  (27 shorter events, 0.5 us)
Async XLA Ops:
  7.2 42.5 %copy-start.4 = (bf16[1,4,32,512]{3,2,1,0:T(8,128)(2,1)S(1)}, bf16[1,4,32,512]{3,2,1,0:T(8,128)(2,1)}, u32[]{:S(2)}) copy-start(bf16[1,4,32,512]{3,2,1,0:T(8,128)(2,1)} %param.5) | copy-start | bytes 393220
  7.2 41.5 %copy-start.3 = (bf16[1,4,32,512]{3,2,1,0:T(8,128)(2,1)S(1)}, bf16[1,4,32,512]{3,2,1,0:T(8,128)(2,1)}, u32[]{:S(2)}) copy-start(bf16[1,4,32,512]{3,2,1,0:T(8,128)(2,1)} %param.6) | copy-start | bytes 393220
  7.2 43.5 %copy-start.2 = (bf16[16,3,3,512]{3,0,2,1:T(8,128)(2,1)S(1)}, bf16[16,3,3,512]{3,0,2,1:T(8,128)(2,1)}, u32[]{:S(2)}) copy-start(bf16[16,3,3,512]{3,0,2,1:T(8,128)(2,1)} %param.7) | copy-start | bytes 442372
  7.2 108.1 %all-gather.2.cloned.1.call-start = ((), (), s32[]{:S(2)}) async-start(), calls=%async_computation.3 | async-start | bytes 12976128 | tf_op jit(solution)/shard_map/all_gather | solution.py:72
  8.2 5.3 %collective-permute-start = (bf16[2,1,1,32,512]{4,3,2,1,0:T(8,128)(2,1)S(1)}, bf16[2,1,1,32,512]{4,3,2,1,0:T(8,128)(2,1)S(1)}, u32[]{:S(2)}, u32[]{:S(2)}) collective-permute-start(bf16[2,1,1,32,512]{4,3,2,1,0:T(8,128)(2,1)S(1)} %get-tuple-element.21), channel_id=1, source_target_pairs={{0,1},{1,2},{2,3},{3,4},{4,5},{5,6},{6,7},{7,8},{8,9},{9,10},{10,1... | collective-permute-start | bytes 196616 | tf_op jit(solution)/shard_map/ppermute | solution.py:15
  11.6 6.2 %collective-permute-start.1 = (bf16[2,1,1,32,512]{4,3,2,1,0:T(8,128)(2,1)S(1)}, bf16[2,1,1,32,512]{4,3,2,1,0:T(8,128)(2,1)S(1)}, u32[]{:S(2)}, u32[]{:S(2)}) collective-permute-start(bf16[2,1,1,32,512]{4,3,2,1,0:T(8,128)(2,1)S(1)} %get-tuple-element.22), channel_id=1, source_target_pairs={{1,0},{2,1},{3,2},{4,3},{5,4},{6,5},{7,6},{8,7},{9,8},{10,9},{11,1... | collective-permute-start | bytes 196616 | tf_op jit(solution)/shard_map/ppermute | solution.py:17
  43.9 8.7 %collective-permute-start.2 = (bf16[2,32,1,32,16]{3,4,2,0,1:T(8,128)(2,1)S(1)}, bf16[2,32,1,32,16]{3,4,2,0,1:T(8,128)(2,1)S(1)}, u32[]{:S(2)}, u32[]{:S(2)}) collective-permute-start(bf16[2,32,1,32,16]{3,4,2,0,1:T(8,128)(2,1)S(1)} %get-tuple-element.15), channel_id=1, source_target_pairs={{0,1},{1,2},{2,3},{3,4},{4,5},{5,6},{6,7},{7,8},{8,9},{9,10},{10,1... | collective-permute-start | bytes 196616 | tf_op jit(solution)/shard_map/ppermute | solution.py:15
  47.3 10.9 %collective-permute-start.3 = (bf16[2,32,1,32,16]{3,4,2,0,1:T(8,128)(2,1)S(1)}, bf16[2,32,1,32,16]{3,4,2,0,1:T(8,128)(2,1)S(1)}, u32[]{:S(2)}, u32[]{:S(2)}) collective-permute-start(bf16[2,32,1,32,16]{3,4,2,0,1:T(8,128)(2,1)S(1)} %get-tuple-element.16), channel_id=1, source_target_pairs={{1,0},{2,1},{3,2},{4,3},{5,4},{6,5},{7,6},{8,7},{9,8},{10,9},{11,1... | collective-permute-start | bytes 196616 | tf_op jit(solution)/shard_map/ppermute | solution.py:17
  180.2 31.5 %all-to-all-start = ((bf16[32,2,2048]{2,1,0:T(2,128)(2,1)}), bf16[32,2,2048]{2,1,0:T(2,128)(2,1)}, u32[]{:S(2)}, u32[]{:S(2)}) async-start(bf16[32,2,2048]{2,1,0:T(2,128)(2,1)} %reshape.100), calls=%async_computation | async-start | bytes 524288 | tf_op jit(solution)/shard_map/all_to_all | solution.py:80
  185.7 124.7 %reduce-scatter.4.cloned.1.call-start = ((), (), s32[]{:S(2)}) async-start(), calls=%async_computation.4 | async-start | bytes 557056
  185.7 9.5 %slice-start = ((s8[12582912]{0:T(1024)(128)(4,1)}), s8[4194304]{0:T(1024)(128)(4,1)S(1)}, s32[]{:S(2)}) async-start(s8[12582912]{0:T(1024)(128)(4,1)} %bitcast.233), calls=%async_computation.5 | async-start | bytes 8388608
  185.7 9.5 %slice-start.1 = ((s8[12582912]{0:T(1024)(128)(4,1)}), s8[4194304]{0:T(1024)(128)(4,1)S(1)}, s32[]{:S(2)}) async-start(s8[12582912]{0:T(1024)(128)(4,1)} %bitcast.233), calls=%async_computation.6 | async-start | bytes 8388608
  190.3 5.2 %slice-start.2 = ((s8[12582912]{0:T(1024)(128)(4,1)}), s8[4194304]{0:T(1024)(128)(4,1)S(1)}, s32[]{:S(2)}) async-start(s8[12582912]{0:T(1024)(128)(4,1)} %bitcast.233), calls=%async_computation.7 | async-start | bytes 8388608
  211.6 2.9 copy-start
  211.6 2.9 copy-start.1
Sparse Core Ops, SparseCore 0:
  19.7 95.5 all-gather.1
  211.8 98.5 reduce-scatter.3
where the time goes:
time: 325 us; the launch traced here: 319 us
  waiting for transfers between devices  162 us (50%)
  matrix products  73.8 us (23%)
  local copies, waits for them, and re-layouts  26.9 us (8%)
  blocking collectives  20.8 us (6%)
  starting transfers between devices  15 us (5%)
  between operations  14.5 us (4%)
  other arithmetic  6.35 us (2%)
    unnamed x3, waiting for transfers between devices  93.8 us
    all_gather x1, waiting for transfers between devices, layer_back(): padded = pad_columns(lax.all_gather(operand, 'img', axis=1, tiled=True))  55.6 us
    dot_general x18, matrix products, tap_product(): lax.dot_general(left, kernel_tap, (((left.ndim - 1,), (1,)), ((), ())), p...  52 us
    dot_general x9, matrix products, weight_terms(): lax.dot_general(window, piece, (((1, 2, 3), (1, 2, 3)), ((0,), (0,))), pr...  21.8 us
    all_to_all x1, blocking collectives, on_device(): lax.all_to_all(stored, 'img', split_axis=4, concat_axis=1, tiled=True)  20.8 us
    unnamed x28, local copies, waits for them, and re-layouts  14.6 us
    squeeze x1, local copies, waits for them, and re-layouts, layer_back(): padded[which]  10.8 us
    ppermute x2, waiting for transfers between devices, with_halo(): lax.ppermute(head, axis, [((i + 1) % count, i) for i in range(ends)])  9.94 us
  transfers between devices with their start and end apart: 7, of which 6 were waited for; matrix products, arithmetic and copies ran while one was open for 12% of the time, Pallas kernels for 0%

commit v1 on v0

--- a/solution.py
+++ b/solution.py
@@ -69,7 +69,11 @@
     batch = inputs_pad.shape[1]
     kernels = (weight, jnp.abs(weight))
     operand = with_halo(upstream, (("rows", 2),), 1)
-    padded = pad_columns(lax.all_gather(operand, "img", axis=1, tiled=True))
+    padded = pad_columns(
+        jnp.concatenate(
+            lax.all_to_all(jnp.stack([operand] * lax.axis_size("img")), "img", 0, 0), axis=1
+        )
+    )
     inner = padded[:, :, 1 : row_count + 1, 1 : col_count + 1, :]
     running = weight_terms(inputs_pad, inner, row_count, col_count)
     fresh = jnp.stack(

time: 325 us -> 560 us (1.72)
  waiting for transfers between devices: 162 us -> 366 us
  blocking collectives: 20.8 us -> 0 us
  matrix products: 73.8 us -> 92.8 us
  starting transfers between devices: 15 us -> 32.8 us
  local copies, waits for them, and re-layouts: 26.9 us -> 39.9 us
    all_to_all x0 -> x2, waiting for transfers between devices: none -> 257 us  [the longest x1 257 us: layer_back(): lax.all_to_all(jnp.stack([operand] * lax.axis_size('img')), 'img', 0, 0)]
    all_gather x1 -> x0, waiting for transfers between devices: 55.6 us -> none  [layer_back(): padded = pad_columns(lax.all_gather(operand, 'img', axis=1, tiled=True))]
    all_to_all x1 -> x0, blocking collectives: 20.8 us -> none  [on_device(): lax.all_to_all(stored, 'img', split_axis=4, concat_axis=1, tiled=True)]
    all_to_all x0 -> x2, starting transfers between devices: none -> 17.9 us  [the longest x1 9.51 us: on_device(): lax.all_to_all(stored, 'img', split_axis=4, concat_axis=1, tiled=True)]
    dot_general x9, matrix products: 21.8 us -> 34.3 us  [weight_terms(): lax.dot_general(window, piece, (((1, 2, 3), (1, 2, 3)), ((0,), (0,))), pr...]
    dot_general x18, matrix products: 52 us -> 58.5 us  [tap_product(): lax.dot_general(left, kernel_tap, (((left.ndim - 1,), (1,)), ((), ())), p...]
    all_to_all x0 -> x1, local copies, waits for them, and re-layouts: none -> 6.23 us  [layer_back(): lax.all_to_all(jnp.stack([operand] * lax.axis_size('img')), 'img', 0, 0)]
    another operation x0 -> x1, local copies, waits for them, and re-layouts: none -> 6.14 us  [layer_back(): jnp.stack([operand] * lax.axis_size('img'))]
  transfers between devices with their start and end apart: 7 -> 8, of which waited for: 6 -> 8; matrix products, arithmetic and copies ran while one was open for 12% -> 4% of each run, Pallas kernels for 0% -> 0%
where the time goes in v1:
time: 560 us; the launch traced here: 552 us
  waiting for transfers between devices  366 us (65%)
  matrix products  92.8 us (17%)
  local copies, waits for them, and re-layouts  39.9 us (7%)
  starting transfers between devices  32.8 us (6%)
  between operations  14.6 us (3%)
  other arithmetic  6.71 us (1%)
    all_to_all x1, waiting for transfers between devices, layer_back(): lax.all_to_all(jnp.stack([operand] * lax.axis_size('img')), 'img', 0, 0)  257 us
    unnamed x2, waiting for transfers between devices  94.5 us
    dot_general x18, matrix products, tap_product(): lax.dot_general(left, kernel_tap, (((left.ndim - 1,), (1,)), ((), ())), p...  58.5 us
    dot_general x9, matrix products, weight_terms(): lax.dot_general(window, piece, (((1, 2, 3), (1, 2, 3)), ((0,), (0,))), pr...  34.3 us
    unnamed x34, local copies, waits for them, and re-layouts  14.9 us
  transfers between devices with their start and end apart: 8, of which 8 were waited for; matrix products, arithmetic and copies ran while one was open for 4% of the time, Pallas kernels for 0%

profile of v1, /device:TPU:8, one launch (start us, length us, event | category | flops | bytes accessed | tf_op | source)
XLA Modules:
  0.0 552.4 jit_solution(7578085973933265606)
XLA Ops:
  7.2 1.0 pad_maximum_fusion.3
  8.2 0.7 copy.27
  8.9 1.7 reshape.113
  10.6 9.5 %all-to-all-start.2 = ((bf16[32,2,2048]{2,1,0:T(2,128)(2,1)}), bf16[32,2,2048]{2,1,0:T(2,128)(2,1)S(1)}, u32[]{:S(2)}, u32[]{:S(2)}) async-start(bf16[32,2,2048]{2,1,0:T(2,128)(2,1)} %reshape.113), calls=%async_computation.2 | async-start | bytes 524288 | tf_op jit(solution)/shard_map/all_to_all | solution.py:92
  20.1 0.8 pad_maximum_fusion.5
  20.9 3.4 collective-permute-start
  24.3 1.3 collective-permute-start.1
  25.6 0.6 collective-permute-done
  26.2 4.3 collective-permute-done.1
  30.5 1.0 maximum_bitcast_fusion
  31.6 6.1 %stack.49 = bf16[32,2,1,6,32,512]{5,4,3,1,2,0:T(8,128)(2,1)} broadcast(bf16[2,6,32,512]{3,2,1,0:T(8,128)(2,1)S(1)} %maximum_bitcast_fusion), dimensions={1,3,4,5} | broadcast | bytes 12976128 | tf_op jit(solution)/shard_map/stack | solution.py:74
  37.8 8.4 %all-to-all-start = ((bf16[32,2,1,6,32,512]{5,4,3,1,2,0:T(8,128)(2,1)}), bf16[32,2,1,6,32,512]{5,4,3,1,2,0:T(8,128)(2,1)}, u32[]{:S(2)}, u32[]{:S(2)}) async-start(bf16[32,2,1,6,32,512]{5,4,3,1,2,0:T(8,128)(2,1)} %stack.49), calls=%async_computation | async-start | bytes 25165824 | tf_op jit(solution)/shard_map/all_to_all | solution.py:74
  46.2 0.5 reshape.114
  47.0 3.4 collective-permute-start.2
  50.4 1.3 collective-permute-start.3
  51.7 1.0 copy.19
  52.8 1.0 copy.20
  53.8 2.4 collective-permute-done.2
  56.3 5.7 %collective-permute-done.3 = bf16[2,32,1,32,16]{3,4,2,0,1:T(8,128)(2,1)S(1)} collective-permute-done((bf16[2,32,1,32,16]{3,4,2,0,1:T(8,128)(2,1)S(1)}, bf16[2,32,1,32,16]{3,4,2,0,1:T(8,128)(2,1)S(1)}, u32[]{:S(2)}, u32[]{:S(2)}) %collective-permute-start.3) | collective-permute-done | bytes 65568 | tf_op jit(solution)/shard_map/ppermute | solution.py:17
  61.9 0.8 fusion.43
  62.8 1.8 multiply_convert_fusion
  64.6 256.8 %all-to-all-done = bf16[32,2,1,6,32,512]{5,4,3,1,2,0:T(8,128)(2,1)} async-done(((bf16[32,2,1,6,32,512]{5,4,3,1,2,0:T(8,128)(2,1)}), bf16[32,2,1,6,32,512]{5,4,3,1,2,0:T(8,128)(2,1)}, u32[]{:S(2)}, u32[]{:S(2)}) %all-to-all-start) | async-done | bytes 12582944 | tf_op jit(solution)/shard_map/all_to_all | solution.py:74
  321.4 6.2 %copy.93 = bf16[32,2,1,6,32,512]{5,4,3,0,1,2:T(8,128)(2,1)S(1)} copy(bf16[32,2,1,6,32,512]{5,4,3,1,2,0:T(8,128)(2,1)} %all-to-all-done) | data formatting | bytes 25165824 | tf_op jit(solution)/shard_map/all_to_all | solution.py:74
  327.7 10.1 %fusion = (bf16[32,6,34,512]{3,2,1,0:T(8,128)(2,1)S(1)}, bf16[32,6,34,512]{3,2,1,0:T(8,128)(2,1)S(1)}) fusion(bf16[2,32,6,32,512]{4,3,2,1,0:T(8,128)(2,1)S(1)} %bitcast.240), kind=kLoop, calls=%fused_computation.3 | loop fusion | bytes 25952256 | tf_op jit(solution)/shard_map/squeeze | solution.py:80
  337.8 3.8 fusion.34
  341.6 2.8 fusion.28
  344.4 2.8 fusion.30
  347.3 2.8 fusion.22
  350.1 2.8 fusion.24
  353.0 4.1 fusion.16
  357.1 2.8 fusion.10
  359.9 2.8 fusion.12
  362.7 2.8 fusion.4
  365.6 3.6 fusion.6
  369.1 3.3 fusion.114
  372.5 3.7 fusion.113
  376.2 4.1 fusion.112
  380.3 3.3 fusion.111
  383.6 3.7 fusion.110
  387.3 3.7 fusion.109
  391.0 3.3 fusion.108
  394.3 3.7 fusion.107
  398.0 4.0 fusion.88
  402.1 2.9 fusion.85
  405.0 2.9 fusion.79
  407.8 3.0 fusion.100
  410.8 3.6 fusion.91
  414.4 3.6 fusion.73
  418.0 3.6 fusion.67
  421.6 3.7 fusion.103
  425.6 1.7 reshape.111
  427.3 5.5 all-to-all-start.1
  432.9 5.4 fusion.106
  438.3 1.1 fusion.171
  439.5 1.5 copy.70
  441.0 2.1 reshape.109
  443.1 1.2 all-to-all-done.1
  444.3 1.9 reshape.112
  447.1 0.4 subtract_convert_fusion
  447.5 0.8 copy.39
  448.3 0.8 copy.40
  449.2 94.5 %reduce-scatter.4.cloned.1.call-done = f32[32,144]{1,0:T(8,128)} async-done(((f32[512,144]{1,0:T(8,128)}), f32[32,144]{1,0:T(8,128)}) %reduce-scatter.4.cloned.1.call-update) | async-done | bytes 18448
  543.7 0.9 reshape.110
  544.6 0.8 copy.71
  (34 shorter events, 1.7 us)
Async XLA Ops:
  10.6 21.0 %all-to-all-start.2 = ((bf16[32,2,2048]{2,1,0:T(2,128)(2,1)}), bf16[32,2,2048]{2,1,0:T(2,128)(2,1)S(1)}, u32[]{:S(2)}, u32[]{:S(2)}) async-start(bf16[32,2,2048]{2,1,0:T(2,128)(2,1)} %reshape.113), calls=%async_computation.2 | async-start | bytes 524288 | tf_op jit(solution)/shard_map/all_to_all | solution.py:92
  20.9 5.3 collective-permute-start
  24.3 6.2 %collective-permute-start.1 = (bf16[2,1,1,32,512]{4,3,2,1,0:T(8,128)(2,1)S(1)}, bf16[2,1,1,32,512]{4,3,2,1,0:T(8,128)(2,1)S(1)}, u32[]{:S(2)}, u32[]{:S(2)}) collective-permute-start(bf16[2,1,1,32,512]{4,3,2,1,0:T(8,128)(2,1)S(1)} %get-tuple-element.22), channel_id=1, source_target_pairs={{1,0},{2,1},{3,2},{4,3},{5,4},{6,5},{7,6},{8,7},{9,8},{10,9},{11,1... | collective-permute-start | bytes 196616 | tf_op jit(solution)/shard_map/ppermute | solution.py:17
  37.8 14.0 %copy-start.7 = (bf16[1,4,32,512]{3,2,1,0:T(8,128)(2,1)S(1)}, bf16[1,4,32,512]{3,2,1,0:T(8,128)(2,1)}, u32[]{:S(2)}) copy-start(bf16[1,4,32,512]{3,2,1,0:T(8,128)(2,1)} %param.6) | copy-start | bytes 393220
  37.8 15.0 %copy-start.8 = (bf16[1,4,32,512]{3,2,1,0:T(8,128)(2,1)S(1)}, bf16[1,4,32,512]{3,2,1,0:T(8,128)(2,1)}, u32[]{:S(2)}) copy-start(bf16[1,4,32,512]{3,2,1,0:T(8,128)(2,1)} %param.5) | copy-start | bytes 393220
  37.8 16.0 %copy-start.5 = (bf16[16,3,3,512]{3,0,2,1:T(8,128)(2,1)S(1)}, bf16[16,3,3,512]{3,0,2,1:T(8,128)(2,1)}, u32[]{:S(2)}) copy-start(bf16[16,3,3,512]{3,0,2,1:T(8,128)(2,1)} %param.7) | copy-start | bytes 442372
  37.8 283.7 %all-to-all-start = ((bf16[32,2,1,6,32,512]{5,4,3,1,2,0:T(8,128)(2,1)}), bf16[32,2,1,6,32,512]{5,4,3,1,2,0:T(8,128)(2,1)}, u32[]{:S(2)}, u32[]{:S(2)}) async-start(bf16[32,2,1,6,32,512]{5,4,3,1,2,0:T(8,128)(2,1)} %stack.49), calls=%async_computation | async-start | bytes 25165824 | tf_op jit(solution)/shard_map/all_to_all | solution.py:74
  47.0 9.3 %collective-permute-start.2 = (bf16[2,32,1,32,16]{3,4,2,0,1:T(8,128)(2,1)S(1)}, bf16[2,32,1,32,16]{3,4,2,0,1:T(8,128)(2,1)S(1)}, u32[]{:S(2)}, u32[]{:S(2)}) collective-permute-start(bf16[2,32,1,32,16]{3,4,2,0,1:T(8,128)(2,1)S(1)} %get-tuple-element.15), channel_id=1, source_target_pairs={{0,1},{1,2},{2,3},{3,4},{4,5},{5,6},{6,7},{7,8},{8,9},{9,10},{10,1... | collective-permute-start | bytes 196616 | tf_op jit(solution)/shard_map/ppermute | solution.py:15
  50.4 11.5 %collective-permute-start.3 = (bf16[2,32,1,32,16]{3,4,2,0,1:T(8,128)(2,1)S(1)}, bf16[2,32,1,32,16]{3,4,2,0,1:T(8,128)(2,1)S(1)}, u32[]{:S(2)}, u32[]{:S(2)}) collective-permute-start(bf16[2,32,1,32,16]{3,4,2,0,1:T(8,128)(2,1)S(1)} %get-tuple-element.16), channel_id=1, source_target_pairs={{1,0},{2,1},{3,2},{4,3},{5,4},{6,5},{7,6},{8,7},{9,8},{10,9},{11,1... | collective-permute-start | bytes 196616 | tf_op jit(solution)/shard_map/ppermute | solution.py:17
  53.8 308.9 %copy-start.9 = (bf16[16,3,3,512]{3,0,2,1:T(8,128)(2,1)}, bf16[16,3,3,512]{3,0,2,1:T(8,128)(2,1)S(1)}, u32[]{:S(2)}) copy-start(bf16[16,3,3,512]{3,0,2,1:T(8,128)(2,1)S(1)} %abs.3) | copy-start | bytes 442372
  327.7 66.6 %copy-start = (bf16[32,2,1,6,32,512]{5,4,3,0,1,2:T(8,128)(2,1)}, bf16[32,2,1,6,32,512]{5,4,3,0,1,2:T(8,128)(2,1)S(1)}, u32[]{:S(2)}) copy-start(bf16[32,2,1,6,32,512]{5,4,3,0,1,2:T(8,128)(2,1)S(1)} %copy.93) | copy-start | bytes 37748740
  405.0 5.9 %copy-start.10 = (f32[32,4,32,16]{2,3,1,0:T(8,128)S(1)}, f32[32,4,32,16]{2,3,1,0:T(8,128)}, u32[]{:S(2)}) copy-start(f32[32,4,32,16]{2,3,1,0:T(8,128)} %fusion.16) | copy-start | bytes 786436
  421.6 11.3 %copy-start.3 = (bf16[1,32,6,34,16]{3,4,2,0,1:T(8,128)(2,1)S(1)}, bf16[1,32,6,34,16]{3,4,2,0,1:T(8,128)(2,1)}, u32[]{:S(2)}) copy-start(bf16[1,32,6,34,16]{3,4,2,0,1:T(8,128)(2,1)} %get-tuple-element.13) | copy-start | bytes 626692
  421.6 11.3 %copy-start.4 = (bf16[1,32,6,34,16]{3,4,2,0,1:T(8,128)(2,1)S(1)}, bf16[1,32,6,34,16]{3,4,2,0,1:T(8,128)(2,1)}, u32[]{:S(2)}) copy-start(bf16[1,32,6,34,16]{3,4,2,0,1:T(8,128)(2,1)} %get-tuple-element.14) | copy-start | bytes 626692
  427.3 17.0 %all-to-all-start.1 = ((bf16[32,2,2048]{2,1,0:T(2,128)(2,1)}), bf16[32,2,2048]{2,1,0:T(2,128)(2,1)}, u32[]{:S(2)}, u32[]{:S(2)}) async-start(bf16[32,2,2048]{2,1,0:T(2,128)(2,1)} %reshape.111), calls=%async_computation.1 | async-start | bytes 524288 | tf_op jit(solution)/shard_map/all_to_all | solution.py:84
  432.8 6.6 %copy-start.6 = (bf16[16,3,3,512]{3,0,2,1:T(8,128)(2,1)S(1)}, bf16[16,3,3,512]{3,0,2,1:T(8,128)(2,1)}, u32[]{:S(2)}) copy-start(bf16[16,3,3,512]{3,0,2,1:T(8,128)(2,1)} %param.7) | copy-start | bytes 442372
  432.8 110.9 %reduce-scatter.4.cloned.1.call-start = ((), (), s32[]{:S(2)}) async-start(), calls=%async_computation.4 | async-start | bytes 557056
  443.1 4.0 copy-start.1
  443.1 4.0 copy-start.2
Sparse Core Ops, SparseCore 0:
  443.2 100.3 reduce-scatter.3
